TPU v7x, 32 devices: a whole 2x2x4 slice. The times are simulated.
32 devices in a mesh: gx: 4 (over y, x), yz: 8 (over z, core).
Axes of the slice: x: 2, y: 2, z: 4, core: 2. Of those that a mesh axis runs over, the one named last changes fastest.
Arguments:
- seg_ends: float32 [6, 131072], P(None, ('gx', 'yz')), may hold values from -6 to 6
- burgers: float32 [3, 131072], P(None, ('gx', 'yz')), may hold values from -6 to 6
- cell_index: int32 [131072], P(('gx', 'yz')), may hold values from 0 to 1023
- send_list: int32 [4, 4096], P(None, ('gx', 'yz')), may hold values from -1 to 4095, as said below
- pair_list: int32 [2, 8192], P(None, ('gx', 'yz')), may hold values from -1 to 35, as said below
- coupling: float32 [6, 9], replicated, may hold values from -2 to 2
Outputs:
- forces: float32 [3, 131072], P(None, ('gx', 'yz'))
Inputs may be any that keep to these rules, and one draw needn't show every extreme that they name: `send_list`: per domain and neighbour, up to 128 distinct rows of 0 to 4095 come first, then -1 in the remaining slots; some list in every draw is full. `pair_list`: per domain, target t < 32 and t <= s < 36, no pair twice; empty slots are -1 in both rows and follow the used ones; some domain fills all 256 slots in every draw.
All inputs are finite; a program needn't handle non-finite values.
Results may differ from a plain program's by a relative error of at most 0.0003.
Values sent between devices are 32-bit elements; how exact they have to be, the bound alone decides.
A program may use at most 64 MiB of HBM per device.

v0:
```python
import jax
import jax.numpy as jnp
from jax import lax
from jax.sharding import PartitionSpec as P

G = 32
TILE = 128
PAIR_BLOCK = 16


far_scale = 0.003
near_scale = 0.25
core_square = 1.0
kernel_spread = 4.0


def passed_along(x, axis, by):
    count = lax.axis_size(axis)
    return lax.ppermute(x, axis, [(i, (i + by) % count) for i in range(count)])


def kernel_rows(first_row, row_count, width):
    rows = first_row + jnp.arange(row_count, dtype=jnp.int32)
    columns = jnp.arange(width, dtype=jnp.int32)
    apart = jnp.abs(rows[:, None] - columns[None, :])
    apart = jnp.minimum(apart, width - apart).astype(jnp.float32)
    return 1.0 / (1.0 + (apart / kernel_spread) ** 2)


def peach_koehler(stress, burgers, tangent):
    push_x = stress[0] * burgers[0] + stress[5] * burgers[1] + stress[4] * burgers[2]
    push_y = stress[5] * burgers[0] + stress[1] * burgers[1] + stress[3] * burgers[2]
    push_z = stress[4] * burgers[0] + stress[3] * burgers[1] + stress[2] * burgers[2]
    return jnp.stack(
        [
            push_y * tangent[2] - push_z * tangent[1],
            push_z * tangent[0] - push_x * tangent[2],
            push_x * tangent[1] - push_y * tangent[0],
        ]
    )


def pair_block(tiles, targets, sources):
    tile_count = tiles.shape[0]
    usable = targets >= 0
    target_safe = jnp.maximum(targets, 0)
    source_safe = jnp.maximum(sources, 0)
    target_rows = tiles[target_safe]
    source_rows = tiles[source_safe]
    target_mid = 0.5 * (target_rows[:, 0:3] + target_rows[:, 3:6])
    source_mid = 0.5 * (source_rows[:, 0:3] + source_rows[:, 3:6])
    offset = target_mid[:, :, :, None] - source_mid[:, :, None, :]
    distance = core_square + jnp.sum(offset * offset, axis=1)
    intersection = jnp.sum(target_rows[:, 6:9, :, None] * source_rows[:, 6:9, None, :], axis=1)
    weight = near_scale * intersection / (distance * jnp.sqrt(distance))
    weight = weight * usable[:, None, None].astype(jnp.float32)
    pushed = weight[:, None] * offset
    on_target = jnp.sum(pushed, axis=3)
    distinct = (targets != sources).astype(jnp.float32)
    on_source = -jnp.sum(pushed, axis=2) * distinct[:, None, None]
    tile_ids = jnp.arange(tile_count, dtype=jnp.int32)
    target_hot = (target_safe[:, None] == tile_ids[None, :]).astype(jnp.float32)
    source_hot = (source_safe[:, None] == tile_ids[None, :]).astype(jnp.float32)
    high = lax.Precision.HIGHEST
    return jnp.einsum("pn,pct->nct", target_hot, on_target, precision=high) + jnp.einsum(
        "pn,pct->nct", source_hot, on_source, precision=high
    )


def ghost_slabs(block, offset_step):
    return passed_along(block, "gx", offset_step)


def ghost_columns(block, offset_step):
    return passed_along(block, "yz", offset_step)


def return_slabs(block, offset_step):
    return passed_along(block, "gx", offset_step)


def return_columns(block, offset_step):
    return passed_along(block, "yz", offset_step)


def on_device(seg_ends, burgers, cell_index, send_list, pair_list, coupling):
    high = lax.Precision.HIGHEST
    slab_count = lax.axis_size("gx")
    column_count = lax.axis_size("yz")
    span_x = G // slab_count
    span_y = G // column_count
    owned = span_x * span_y * G
    seg_count = seg_ends.shape[1]
    local_tiles = seg_count // TILE
    tangent = seg_ends[3:6] - seg_ends[0:3]
    moment_terms = (burgers[:, None, :] * tangent[None, :, :]).reshape(9, seg_count)
    local_moments = jax.ops.segment_sum(moment_terms.T, cell_index, num_segments=owned).T
    slab_start = lax.axis_index("gx") * span_x
    column_start = lax.axis_index("yz") * span_y
    slab_rows = kernel_rows(slab_start, span_x, G)
    column_rows = kernel_rows(column_start, span_y, G)
    depth_rows = kernel_rows(0, G, G)
    placed = lax.dynamic_update_slice(
        jnp.zeros((9, G, G, G), jnp.float32),
        local_moments.reshape(9, span_x, span_y, G),
        (0, slab_start, column_start, 0),
    )
    full_grid = lax.psum(placed, ("gx", "yz"))
    along_x = jnp.einsum("xa,kabc->kxbc", slab_rows, full_grid, precision=high)
    along_y = jnp.einsum("yb,kxbc->kxyc", column_rows, along_x, precision=high)
    along_z = jnp.einsum("zc,kxyc->kxyz", depth_rows, along_y, precision=high)
    stress = far_scale * jnp.dot(coupling, along_z.reshape(9, owned), precision=high)
    far_force = peach_koehler(jnp.take(stress, cell_index, axis=1), burgers, tangent)
    segment_data = jnp.concatenate([seg_ends, burgers], axis=0)
    usable = (send_list >= 0).astype(jnp.float32)
    safe_rows = jnp.maximum(send_list, 0)
    outgoing = jnp.take(segment_data, safe_rows, axis=1) * usable[None]
    ghosts = jnp.stack(
        [
            ghost_slabs(outgoing[:, 0], 1),
            ghost_slabs(outgoing[:, 1], -1),
            ghost_columns(outgoing[:, 2], 1),
            ghost_columns(outgoing[:, 3], -1),
        ]
    )
    local_blocks = segment_data.reshape(9, local_tiles, TILE).transpose(1, 0, 2)
    tiles = jnp.concatenate([local_blocks, ghosts], axis=0)

    def accumulate(block_index, totals):
        targets = lax.dynamic_slice_in_dim(pair_list[0], block_index * PAIR_BLOCK, PAIR_BLOCK)
        sources = lax.dynamic_slice_in_dim(pair_list[1], block_index * PAIR_BLOCK, PAIR_BLOCK)
        return totals + pair_block(tiles, targets, sources)

    empty = jnp.zeros((local_tiles + 4, 3, TILE), jnp.float32)
    totals = lax.fori_loop(0, pair_list.shape[1] // PAIR_BLOCK, accumulate, empty)
    near_force = totals[:local_tiles].transpose(1, 0, 2).reshape(3, seg_count)
    returned = jnp.stack(
        [
            return_slabs(totals[local_tiles], -1),
            return_slabs(totals[local_tiles + 1], 1),
            return_columns(totals[local_tiles + 2], -1),
            return_columns(totals[local_tiles + 3], 1),
        ]
    )
    returned = returned * usable[:, None, :]
    back_force = (
        jnp.zeros((3, seg_count), jnp.float32)
        .at[:, safe_rows.reshape(-1)]
        .add(returned.transpose(1, 0, 2).reshape(3, 4 * TILE))
    )
    return far_force + near_force + back_force


def solution(mesh):
    placed = (
        P(None, ("gx", "yz")),
        P(None, ("gx", "yz")),
        P(("gx", "yz")),
        P(None, ("gx", "yz")),
        P(None, ("gx", "yz")),
        P(),
    )
    return jax.shard_map(
        on_device, mesh=mesh, in_specs=placed, out_specs=P(None, ("gx", "yz")), check_vma=False
    )
```

profile of v0, /device:TPU:0, one launch (start us, length us, event | category | flops | bytes accessed | tf_op | source)
XLA Modules:
  0.0 218.2 jit_solution(7308851553740527706)
XLA Ops:
  9.2 22.5 %scatter_custom_fusion = f32[1024,9]{1,0:T(8,128)S(1)} fusion(s32[4096]{0:T(1024)S(1)} %copy-done.3, f32[4096,9]{1,0:T(8,128)S(1)} %copy.194, f32[]{:T(128)} %constant.123.clone.1), kind=kCustom, calls=%fused_computation.53 | custom fusion | flops 36864 | bytes 36868 | tf_op jit(solution)/shard_map/scatter-add | solution.py:97
  32.0 2.8 %broadcast_in_dim.86 = f32[9,32,32,32]{3,1,2,0:T(8,128)} broadcast(f32[]{:T(128)} %constant.123.clone.1), dimensions={} | broadcast | bytes 1179652 | tf_op jit(solution)/shard_map/broadcast_in_dim | solution.py:104
  38.3 3.0 %collective-permute-start = (f32[9,128]{1,0:T(8,128)S(1)}, f32[9,128]{1,0:T(8,128)S(1)}, u32[]{:S(2)}, u32[]{:S(2)}) collective-permute-start(f32[9,128]{1,0:T(8,128)S(1)} %get-tuple-element.131), channel_id=1, source_target_pairs={{0,8},{8,16},{16,24},{24,0},{1,9},{9,17},{17,25},{25,1},{2,10},{10... | collective-permute-start | bytes 13832 | tf_op jit(solution)/shard_map/ppermute | solution.py:19
  42.3 3.5 %collective-permute-start.3 = (f32[9,128]{1,0:T(8,128)S(1)}, f32[9,128]{1,0:T(8,128)S(1)}, u32[]{:S(2)}, u32[]{:S(2)}) collective-permute-start(f32[9,128]{1,0:T(8,128)S(1)} %get-tuple-element.128), channel_id=1, source_target_pairs={{0,7},{1,0},{2,1},{3,2},{4,3},{5,4},{6,5},{7,6},{8,15},{9,8},{10,9... | collective-permute-start | bytes 13832 | tf_op jit(solution)/shard_map/ppermute | solution.py:19
  46.2 1.1 collective-permute-done.2
  47.3 106.0 %while.14 = (s32[]{:T(128)}, f32[36,3,128]{2,0,1:T(8,128)S(1)}, s32[2,256]{1,0:T(2,128)S(1)}, f32[36,9,128]{2,1,0:T(8,128)S(1)}, s32[]{:T(128)}, /*index=5*/s32[]{:T(128)}, s32[]{:T(128)}, s32[]{:T(128)}) while((s32[]{:T(128)}, f32[36,3,128]{2,0,1:T(8,128)S(1)}, s32[2,256]{1,0:T(2,128)S(1)}, f32[36,9,128]{2,1,0:T(8,128)S(1)}, ...), condition=%wide.region_7.8_spmd.clone, body=%wide.region_2.7_spmd.clone.sunk | while | flops 13242087 | bytes 7312541 | solution.py:135
  51.3 2.0 fusion.122
  57.9 2.0 fusion.122
  64.6 2.0 fusion.122
  71.2 2.0 fusion.122
  77.8 2.0 fusion.122
  84.4 2.0 fusion.122
  91.0 2.0 fusion.122
  97.7 2.0 fusion.122
  104.3 2.0 fusion.122
  110.9 2.0 fusion.122
  117.5 2.0 fusion.122
  124.2 2.0 fusion.122
  130.8 2.0 fusion.122
  137.4 2.0 fusion.122
  144.0 2.0 fusion.122
  150.6 2.0 fusion.122
  154.0 3.0 %collective-permute-start.6 = (f32[3,128]{1,0:T(4,128)S(1)}, f32[3,128]{1,0:T(4,128)S(1)}, u32[]{:S(2)}, u32[]{:S(2)}) collective-permute-start(f32[3,128]{1,0:T(4,128)S(1)} %get-tuple-element.127), channel_id=1, source_target_pairs={{0,7},{1,0},{2,1},{3,2},{4,3},{5,4},{6,5},{7,6},{8,15},{9,8},{10,9... | collective-permute-start | bytes 4616 | tf_op jit(solution)/shard_map/ppermute | solution.py:19
  158.0 1.9 collective-permute-start.4
  159.9 2.0 copy.205
  162.2 21.2 %all-reduce.2.cloned.1.call-done = f32[9,32,32,32]{3,1,2,0:T(8,128)} async-done(((f32[9,32,32,32]{3,1,2,0:T(8,128)}), f32[9,32,32,32]{3,1,2,0:T(8,128)}) %all-reduce.2.cloned.1.call-update) | async-done | bytes 1179664 | tf_op jit(solution)/shard_map/psum | solution.py:108
  183.4 4.4 %convolution_bitcast_fusion = f32[9,8,32,32]{3,1,2,0:T(8,128)S(1)} fusion(f32[9,32,32,32]{3,1,2,0:T(8,128)} %all-reduce.2.cloned.1.call-done, s32[8]{0:T(128)S(1)} %iota_add_fusion.1), kind=kOutput, calls=%fused_computation.43 | convolution fusion | flops 28313856 | bytes 1474592 | tf_op jit(solution)/shard_map/xa,kabc->kxbc/dot_general | solution.py:109
  189.6 10.8 %gather_fusion.2 = f32[4096,6]{1,0:T(8,128)S(1)} fusion(f32[6,1024]{0,1:T(8,128)S(1)} %copy.200, s32[4096]{0:T(1024)S(1)} %fusion.47), kind=kCustom, calls=%fused_computation.2 | custom fusion | bytes 212992 | tf_op jit(solution)/shard_map/jit(_take)/gather | solution.py:113
  201.4 2.0 copy.206
  203.4 2.4 %bitcast_add_fusion = f32[3,4096]{0,1:T(8,128)S(1)} fusion(f32[3,4096]{0,1:T(8,128)} %copy.206, f32[3,32,128]{0,2,1:T(8,128)} %copy.205), kind=kLoop, calls=%fused_computation.42 | loop fusion | flops 12288 | bytes 147456 | tf_op jit(solution)/shard_map/add | solution.py:151
  205.8 4.3 %scatter_fusion = f32[3,4096]{0,1:T(8,128)S(1)} fusion(f32[3,4096]{0,1:T(8,128)S(1)} %bitcast_add_fusion, s32[512]{0:T(512)S(1)} %bitcast.108, f32[512,3]{1,0:T(8,128)S(1)} %copy.210), kind=kCustom, calls=%fused_computation.5 | custom fusion | flops 1536 | bytes 20480 | tf_op jit(solution)/shard_map/scatter-add | solution.py:149
  210.1 1.2 copy.211
  (296 shorter events, 84.0 us)
Async XLA Ops:
  6.5 182.7 %copy-start = (f32[6,9]{1,0:T(8,128)S(1)}, f32[6,9]{1,0:T(8,128)}, u32[]{:S(2)}) copy-start(f32[6,9]{1,0:T(8,128)} %param.13) | copy-start | bytes 652
  6.5 2.7 %copy-start.3 = (s32[4096]{0:T(1024)S(1)}, s32[4096]{0:T(1024)}, u32[]{:S(2)}) copy-start(s32[4096]{0:T(1024)} %param.10) | copy-start | bytes 49156
  6.5 176.8 %all-reduce.2.cloned.1.call-start = ((), (), s32[]{:S(2)}) async-start(), calls=%async_computation | async-start | bytes 9437184 | tf_op jit(solution)/shard_map/psum | solution.py:108
  35.4 0.8 copy-start.1
  35.4 0.9 copy-start.2
  35.4 1.0 copy-start.5
  36.4 10.9 %copy-start.4 = (s32[2,256]{1,0:T(2,128)S(1)}, s32[2,256]{1,0:T(2,128)}, u32[]{:S(2)}) copy-start(s32[2,256]{1,0:T(2,128)} %param.12) | copy-start | bytes 6148
  38.3 7.8 %collective-permute-start = (f32[9,128]{1,0:T(8,128)S(1)}, f32[9,128]{1,0:T(8,128)S(1)}, u32[]{:S(2)}, u32[]{:S(2)}) collective-permute-start(f32[9,128]{1,0:T(8,128)S(1)} %get-tuple-element.131), channel_id=1, source_target_pairs={{0,8},{8,16},{16,24},{24,0},{1,9},{9,17},{17,25},{25,1},{2,10},{10... | collective-permute-start | bytes 13832 | tf_op jit(solution)/shard_map/ppermute | solution.py:19
  41.3 4.9 %collective-permute-start.1 = (f32[9,128]{1,0:T(8,128)S(1)}, f32[9,128]{1,0:T(8,128)S(1)}, u32[]{:S(2)}, u32[]{:S(2)}) collective-permute-start(f32[9,128]{1,0:T(8,128)S(1)} %get-tuple-element.130), channel_id=1, source_target_pairs={{0,24},{8,0},{16,8},{24,16},{1,25},{9,1},{17,9},{25,17},{2,26},{10... | collective-permute-start | bytes 13832 | tf_op jit(solution)/shard_map/ppermute | solution.py:19
  42.3 5.0 %collective-permute-start.2 = (f32[9,128]{1,0:T(8,128)S(1)}, f32[9,128]{1,0:T(8,128)S(1)}, u32[]{:S(2)}, u32[]{:S(2)}) collective-permute-start(f32[9,128]{1,0:T(8,128)S(1)} %get-tuple-element.129), channel_id=1, source_target_pairs={{0,1},{1,2},{2,3},{3,4},{4,5},{5,6},{6,7},{7,0},{8,9},{9,10},{10,1... | collective-permute-start | bytes 13832 | tf_op jit(solution)/shard_map/ppermute | solution.py:19
  42.3 5.0 %collective-permute-start.3 = (f32[9,128]{1,0:T(8,128)S(1)}, f32[9,128]{1,0:T(8,128)S(1)}, u32[]{:S(2)}, u32[]{:S(2)}) collective-permute-start(f32[9,128]{1,0:T(8,128)S(1)} %get-tuple-element.128), channel_id=1, source_target_pairs={{0,7},{1,0},{2,1},{3,2},{4,3},{5,4},{6,5},{7,6},{8,15},{9,8},{10,9... | collective-permute-start | bytes 13832 | tf_op jit(solution)/shard_map/ppermute | solution.py:19
  153.4 8.5 %collective-permute-start.7 = (f32[3,128]{1,0:T(4,128)S(1)}, f32[3,128]{1,0:T(4,128)S(1)}, u32[]{:S(2)}, u32[]{:S(2)}) collective-permute-start(f32[3,128]{1,0:T(4,128)S(1)} %get-tuple-element.126), channel_id=1, source_target_pairs={{0,1},{1,2},{2,3},{3,4},{4,5},{5,6},{6,7},{7,0},{8,9},{9,10},{10,1... | collective-permute-start | bytes 4616 | tf_op jit(solution)/shard_map/ppermute | solution.py:19
  154.0 7.9 %collective-permute-start.6 = (f32[3,128]{1,0:T(4,128)S(1)}, f32[3,128]{1,0:T(4,128)S(1)}, u32[]{:S(2)}, u32[]{:S(2)}) collective-permute-start(f32[3,128]{1,0:T(4,128)S(1)} %get-tuple-element.127), channel_id=1, source_target_pairs={{0,7},{1,0},{2,1},{3,2},{4,3},{5,4},{6,5},{7,6},{8,15},{9,8},{10,9... | collective-permute-start | bytes 4616 | tf_op jit(solution)/shard_map/ppermute | solution.py:19
  157.0 4.9 %collective-permute-start.5 = (f32[3,128]{1,0:T(4,128)S(1)}, f32[3,128]{1,0:T(4,128)S(1)}, u32[]{:S(2)}, u32[]{:S(2)}) collective-permute-start(f32[3,128]{1,0:T(4,128)S(1)} %bitcast.114), channel_id=1, source_target_pairs={{0,8},{8,16},{16,24},{24,0},{1,9},{9,17},{17,25},{25,1},{2,10},{10... | collective-permute-start | bytes 4616 | tf_op jit(solution)/shard_map/ppermute | solution.py:19
  158.0 4.0 %collective-permute-start.4 = (f32[3,128]{1,0:T(4,128)S(1)}, f32[3,128]{1,0:T(4,128)S(1)}, u32[]{:S(2)}, u32[]{:S(2)}) collective-permute-start(f32[3,128]{1,0:T(4,128)S(1)} %get-tuple-element.125), channel_id=1, source_target_pairs={{0,24},{8,0},{16,8},{24,16},{1,25},{9,1},{17,9},{25,17},{2,26},{10... | collective-permute-start | bytes 4616 | tf_op jit(solution)/shard_map/ppermute | solution.py:19
Sparse Core Ops, SparseCore 0:
  35.6 147.7 all-reduce.1
where the time goes:
time: 218 us
  other arithmetic  108 us (50%)
  local copies, waits for them, and re-layouts  42.7 us (20%)
  waiting for transfers between devices  22.5 us (10%)
  matrix products  15.2 us (7%)
  starting transfers between devices  14.2 us (7%)
  between operations  13.8 us (6%)
    reduce_sum x16, other arithmetic, pair_block(): on_source = -jnp.sum(pushed, axis=2) * distinct[:, None, None]  32.4 us
    scatter-add x1, other arithmetic, on_device(): jax.ops.segment_sum(moment_terms.T, cell_index, num_segments=owned)  22.5 us
    psum x1, waiting for transfers between devices, on_device(): full_grid = lax.psum(placed, ('gx', 'yz'))  21.2 us
    reduce_sum x16, other arithmetic, pair_block(): distance = core_square + jnp.sum(offset * offset, axis=1)  16.7 us
    reduce_sum x16, other arithmetic, pair_block(): jnp.sum(target_rows[:, 6:9, :, None] * source_rows[:, 6:9, None, :], axis=1)  16.6 us
    ppermute x8, starting transfers between devices, passed_along(): return lax.ppermute(x, axis, [(i, (i + by) % count) for i in range(count)])  14.1 us
    gather x2, local copies, waits for them, and re-layouts, on_device(): jnp.take(stress, cell_index, axis=1)  11.4 us
    gather x16, local copies, waits for them, and re-layouts, pair_block(): target_rows = tiles[target_safe]  9.04 us
  transfers between devices with their start and end apart: 9, of which 3 were waited for; matrix products, arithmetic and copies ran while one was open for 50% of the time, Pallas kernels for 0%

commit v1 on v0

v1 whole, which is shorter than its diff:
```python
import functools

import jax
import jax.numpy as jnp
import numpy as np
from jax import lax
from jax.experimental import pallas as pl
from jax.experimental.pallas import tpu as pltpu
from jax.sharding import PartitionSpec as P

G = 32
TILE = 128
LANES = 128
TOGETHER = 8
CHUNK = 512

far_scale = 0.003
near_scale = 0.25
core_square = 1.0
kernel_spread = 4.0

MESH = pl.DeviceIdType.MESH
f32 = jnp.float32
bf16 = jnp.bfloat16
NT = (((1,), (1,)), ((), ()))
NN = (((1,), (0,)), ((), ()))


def kernel_of(apart):
    apart = np.abs(apart) % G
    apart = np.minimum(apart, G - apart).astype(np.float32)
    return (1.0 / (1.0 + (apart / np.float32(kernel_spread)) ** 2)).astype(np.float32)


def column_matrices(column_count, span_y):
    cells = span_y * G
    width = -(-cells // LANES) * LANES
    at = np.arange(cells)
    result = np.zeros((column_count, width, width), np.float32)
    for slot in range(column_count):
        from_y = slot * span_y + at // G
        result[slot, :cells, :cells] = kernel_of(from_y[:, None] - (at // G)[None, :]) * kernel_of(
            (at % G)[:, None] - (at % G)[None, :]
        )
    return result


def slab_matrices(slab_count, span_x):
    at = np.arange(span_x)
    result = []
    for slot in range(slab_count):
        along = kernel_of((slot * span_x + at)[None, :] - at[:, None]) * np.float32(far_scale)
        result.append(np.kron(along, np.eye(8, dtype=np.float32)))
    return np.stack(result).astype(np.float32)


def pieces_of(x):
    first = x.astype(bf16).astype(f32)
    rest = x - first
    second = rest.astype(bf16).astype(f32)
    return first, second, rest - second


def dot(a, b, dims=NN):
    return lax.dot_general(a, b, dims, preferred_element_type=f32)


def dot_high(a, b):
    return lax.dot_general(a, b, NN, precision=lax.Precision.HIGHEST, preferred_element_type=f32)


def body(
    span_x,
    span_y,
    slab_count,
    column_count,
    seg_ref,
    burgers_ref,
    cell_ref,
    send_ref,
    pair_ref,
    pair_smem,
    coupling_ref,
    column_ref,
    slab_ref,
    out_ref,
    raw,
    ghost_out,
    ghost_in,
    left_ops,
    right_ops,
    mid_ops,
    hot_cells,
    moments,
    column_slots,
    slab_slots,
    stress,
    pushed,
    return_out,
    return_in,
    ghost_send,
    ghost_recv,
    column_send,
    column_recv,
    slab_send,
    slab_recv,
    return_send,
    return_recv,
):
    seg_count = seg_ref.shape[1]
    local_tiles = seg_count // TILE
    pair_count = pair_ref.shape[1]
    cells = span_y * G
    width = column_ref.shape[1]
    gx = lax.axis_index("gx")
    yz = lax.axis_index("yz")

    def slab_peer(by):
        return (lax.rem(gx + by, slab_count), yz)

    def column_peer(by):
        return (gx, lax.rem(yz + by, column_count))

    barrier = pltpu.get_barrier_semaphore()
    for by in range(1, slab_count):
        pl.semaphore_signal(barrier, inc=1, device_id=slab_peer(by), device_id_type=MESH)
    for by in range(1, column_count):
        pl.semaphore_signal(barrier, inc=1, device_id=column_peer(by), device_id_type=MESH)

    raw[...] = jnp.zeros_like(raw)
    for tile in range(local_tiles):
        at = slice(tile * TILE, (tile + 1) * TILE)
        raw[tile, 0:3] = 0.5 * (seg_ref[0:3, at] + seg_ref[3:6, at])
        raw[tile, 8:11] = burgers_ref[0:3, at]

    sub = lax.broadcasted_iota(jnp.int32, (TILE, 4 * TILE), 0)
    rows = jnp.concatenate([send_ref[n : n + 1, :] for n in range(4)], axis=1)
    row_tile = rows >> 7
    hot_rows = jnp.where(sub == (rows & 127), 1.0, 0.0).astype(bf16)
    flat = raw[0:local_tiles].reshape(local_tiles * 16, TILE)
    first, second, third = (piece.astype(bf16) for piece in pieces_of(flat))
    picked = dot(first, hot_rows) + dot(second, hot_rows) + dot(third, hot_rows)
    outgoing = jnp.zeros((16, 4 * TILE), f32)
    for tile in range(local_tiles):
        outgoing = outgoing + jnp.where(row_tile == tile, picked[tile * 16 : (tile + 1) * 16], 0.0)
    for n in range(4):
        ghost_out[n] = outgoing[:, n * TILE : (n + 1) * TILE]

    pl.semaphore_wait(barrier, slab_count - 1 + column_count - 1)

    onward = [
        slab_peer(1),
        slab_peer(slab_count - 1),
        column_peer(1),
        column_peer(column_count - 1),
    ]
    backward = [onward[1], onward[0], onward[3], onward[2]]
    ghost_copies = []
    for n in range(4):
        copy = pltpu.make_async_remote_copy(
            src_ref=ghost_out.at[n],
            dst_ref=ghost_in.at[n],
            send_sem=ghost_send.at[n],
            recv_sem=ghost_recv.at[n],
            device_id=onward[n],
            device_id_type=MESH,
        )
        copy.start()
        ghost_copies.append(copy)

    moments[...] = jnp.zeros_like(moments)

    @pl.loop(0, seg_count // CHUNK)
    def _(step):
        at = pl.ds(pl.multiple_of(step * CHUNK, CHUNK), CHUNK)
        cell = cell_ref[:, at]
        high = cell // cells
        low = cell - high * cells
        hot = jnp.where(lax.broadcasted_iota(jnp.int32, (width, CHUNK), 0) == low, 1.0, 0.0).astype(bf16)
        hot_cells[:, at] = hot
        tangent = seg_ref[3:6, at] - seg_ref[0:3, at]
        vector = burgers_ref[:, at]
        terms = jnp.concatenate(
            [vector[a : a + 1] * tangent for a in range(3)] + [jnp.zeros((7, CHUNK), f32)], axis=0
        )
        stacked = []
        for piece in pieces_of(terms):
            for x in range(span_x):
                stacked.append(jnp.where(high == x, piece, 0.0).astype(bf16))
        moments[...] += dot(jnp.concatenate(stacked, axis=0), hot, NT)

    count = span_x * 16
    summed = moments[0:count] + moments[count : 2 * count] + moments[2 * count : 3 * count]
    column_slots[0] = jnp.zeros_like(column_slots[0])
    for x in range(span_x):
        total = jnp.zeros((6, width), f32)
        for k in range(9):
            total = total + coupling_ref[:, k : k + 1] * summed[x * 16 + k : x * 16 + k + 1]
        column_slots[0, x * 8 : x * 8 + 6] = total

    column_copies = []
    for by in range(1, column_count):
        copy = pltpu.make_async_remote_copy(
            src_ref=column_slots.at[0],
            dst_ref=column_slots.at[column_count - by],
            send_sem=column_send.at[by],
            recv_sem=column_recv.at[column_count - by],
            device_id=column_peer(by),
            device_id_type=MESH,
        )
        copy.start()
        column_copies.append(copy)

    eight = lax.broadcasted_iota(jnp.int32, (8, TILE), 0)

    def spread(a, b, c, low):
        picked = jnp.where(eight == low, a, 0.0)
        picked = jnp.where(eight == low + 1, b, picked)
        picked = jnp.where(eight == low + 2, c, picked)
        other = 3 - low
        return jnp.where((eight >= other) & (eight < other + 3), 1.0, picked)

    def prepare(tile, data):
        mid, vector = data[0:8], data[8:16]
        m1, m2, m3 = pieces_of(mid)
        b1, b2, b3 = pieces_of(vector)
        norm = jnp.sum(mid * mid, axis=0, keepdims=True)
        none = jnp.zeros((8, TILE), f32)
        left_norm = spread(*pieces_of(norm + core_square), 0)
        right_norm = spread(*pieces_of(norm), 3)
        left = [-2.0 * m1, -2.0 * m1, -2.0 * m2, -2.0 * m2, -2.0 * m1, -2.0 * m3, left_norm]
        left += [near_scale * b for b in (b1, b1, b2, b2, b1, b3)] + [none] * 3
        left_ops[tile] = jnp.concatenate(left, axis=0).T.astype(bf16)
        far_half = jnp.concatenate([m1, m2, m1, m2, m3, m1, right_norm] + [none] * 9, axis=0)
        dot_half = jnp.concatenate([none] * 7 + [b1, b2, b1, b2, b3, b1] + [none] * 3, axis=0)
        right_ops[tile, :, 0:TILE] = far_half.astype(bf16)
        right_ops[tile, :, TILE : 2 * TILE] = dot_half.astype(bf16)
        mids = jnp.concatenate([m1, m2, m3, jnp.ones((8, TILE), f32)], axis=0).astype(bf16)
        mid_ops[tile, :, 0:TILE] = mids
        mid_ops[tile, :, TILE : 2 * TILE] = mids

    @pl.loop(0, local_tiles // 4)
    def _(step):
        for k in range(4):
            prepare(step * 4 + k, raw[step * 4 + k])

    for n in range(4):
        ghost_copies[n].wait()
        data = ghost_in[n]
        raw[local_tiles + n] = data
        prepare(local_tiles + n, data)

    def pairs(step):
        base = step * TOGETHER
        targets = [jnp.maximum(pair_smem[0, base + k], 0) for k in range(TOGETHER)]
        sources = [jnp.maximum(pair_smem[1, base + k], 0) for k in range(TOGETHER)]
        both = [dot(left_ops[targets[k]], right_ops[sources[k]]) for k in range(TOGETHER)]
        for k in range(TOGETHER):
            near = lax.rsqrt(both[k][:, 0:TILE])
            weight = both[k][:, TILE : 2 * TILE] * (near * near * near)
            coarse = weight.astype(bf16)
            fine = (weight - coarse.astype(f32)).astype(bf16)
            on_target = dot(mid_ops[sources[k]], jnp.concatenate([coarse, fine], axis=1), NT)
            on_source = dot(mid_ops[targets[k]], jnp.concatenate([coarse, fine], axis=0))
            for side, tile, got in ((0, targets[k], on_target), (1, sources[k], on_source)):
                force = raw[tile][0:8] * got[24:32] - (got[0:8] + got[8:16] + got[16:24])
                for c in range(3):
                    pushed[c, pl.ds(side * pair_count + base + k, 1)] = force[c : c + 1]

    steps = pair_count // TOGETHER
    pl.loop(0, steps // 2)(pairs)

    for copy in column_copies:
        copy.wait()
    along = dot_high(column_slots[0], column_ref[0])
    for slot in range(1, column_count):
        along = along + dot_high(column_slots[slot], column_ref[slot])
    slab_slots[0] = along
    slab_copies = []
    for by in range(1, slab_count):
        copy = pltpu.make_async_remote_copy(
            src_ref=slab_slots.at[0],
            dst_ref=slab_slots.at[slab_count - by],
            send_sem=slab_send.at[by],
            recv_sem=slab_recv.at[slab_count - by],
            device_id=slab_peer(by),
            device_id_type=MESH,
        )
        copy.start()
        slab_copies.append(copy)

    pl.loop(steps // 2, steps)(pairs)

    tile_rows = -(-(local_tiles + 4) // 16) * 16
    ids = lax.broadcasted_iota(jnp.int32, (tile_rows, pair_count), 0)
    targets = pair_ref[0:1, :]
    sources = pair_ref[1:2, :]
    to_target = jnp.where(ids == targets, 1.0, 0.0)
    to_source = jnp.where((ids == sources) & (targets != sources), 1.0, 0.0)
    to_tile = jnp.concatenate([to_target, to_source], axis=1).astype(bf16)
    near = []
    for c in range(3):
        first, second, third = (piece.astype(bf16) for piece in pieces_of(pushed[c]))
        near.append(dot(to_tile, first) + dot(to_tile, second) + dot(to_tile, third))
    return_out[...] = jnp.zeros_like(return_out)
    return_copies = []
    for n in range(4):
        for c in range(3):
            return_out[n, c : c + 1] = near[c][local_tiles + n : local_tiles + n + 1]
        copy = pltpu.make_async_remote_copy(
            src_ref=return_out.at[n],
            dst_ref=return_in.at[n],
            send_sem=return_send.at[n],
            recv_sem=return_recv.at[n],
            device_id=backward[n],
            device_id_type=MESH,
        )
        copy.start()
        return_copies.append(copy)

    for copy in slab_copies:
        copy.wait()
    along = dot_high(slab_ref[0], slab_slots[0])
    for slot in range(1, slab_count):
        along = along + dot_high(slab_ref[slot], slab_slots[slot])
    stress[...] = jnp.concatenate([piece.astype(bf16) for piece in pieces_of(along)], axis=0)

    @pl.loop(0, seg_count // CHUNK)
    def _(step):
        at = pl.ds(pl.multiple_of(step * CHUNK, CHUNK), CHUNK)
        high = cell_ref[:, at] // cells
        count = span_x * 8
        got = dot(stress[...], hot_cells[:, at])
        got = got[0:count] + got[count : 2 * count] + got[2 * count : 3 * count]
        s = jnp.zeros((8, CHUNK), f32)
        for x in range(span_x):
            s = s + jnp.where(high == x, got[x * 8 : (x + 1) * 8], 0.0)
        t = seg_ref[3:6, at] - seg_ref[0:3, at]
        b = burgers_ref[:, at]
        push_x = s[0:1] * b[0:1] + s[5:6] * b[1:2] + s[4:5] * b[2:3]
        push_y = s[5:6] * b[0:1] + s[1:2] * b[1:2] + s[3:4] * b[2:3]
        push_z = s[4:5] * b[0:1] + s[3:4] * b[1:2] + s[2:3] * b[2:3]
        out_ref[0:1, at] = push_y * t[2:3] - push_z * t[1:2]
        out_ref[1:2, at] = push_z * t[0:1] - push_x * t[2:3]
        out_ref[2:3, at] = push_x * t[1:2] - push_y * t[0:1]

    for copy in return_copies:
        copy.wait()
    returned = jnp.concatenate([return_in[n] for n in range(4)], axis=1)
    back = None
    for piece in pieces_of(returned):
        parts = [jnp.where(row_tile == tile, piece, 0.0) for tile in range(local_tiles)]
        term = dot(jnp.concatenate(parts, axis=0).astype(bf16), hot_rows, NT)
        back = term if back is None else back + term
    for tile in range(local_tiles):
        at = slice(tile * TILE, (tile + 1) * TILE)
        for c in range(3):
            out_ref[c : c + 1, at] += (
                near[c][tile : tile + 1] + back[tile * 8 + c : tile * 8 + c + 1]
            )


def on_device(seg_ends, burgers, cell_index, send_list, pair_list, coupling):
    slab_count = lax.axis_size("gx")
    column_count = lax.axis_size("yz")
    span_x = G // slab_count
    span_y = G // column_count
    seg_count = seg_ends.shape[1]
    tiles = seg_count // TILE + 4
    columns = jnp.asarray(column_matrices(column_count, span_y))
    slabs = jnp.asarray(slab_matrices(slab_count, span_x))
    width = columns.shape[1]
    vmem = pl.BlockSpec(memory_space=pltpu.VMEM)
    smem = pl.BlockSpec(memory_space=pltpu.SMEM)
    sems = pltpu.SemaphoreType.DMA
    return pl.pallas_call(
        functools.partial(body, span_x, span_y, slab_count, column_count),
        out_shape=jax.ShapeDtypeStruct((3, seg_count), f32),
        in_specs=[vmem] * 5 + [smem] + [vmem] * 3,
        out_specs=vmem,
        scratch_shapes=[
            pltpu.VMEM((tiles - 4 + 4, 16, TILE), f32),
            pltpu.VMEM((4, 16, TILE), f32),
            pltpu.VMEM((4, 16, TILE), f32),
            pltpu.VMEM((tiles, TILE, TILE), bf16),
            pltpu.VMEM((tiles, TILE, 2 * TILE), bf16),
            pltpu.VMEM((tiles, 32, 2 * TILE), bf16),
            pltpu.VMEM((width, seg_count), bf16),
            pltpu.VMEM((3 * span_x * 16, width), f32),
            pltpu.VMEM((column_count, span_x * 8, width), f32),
            pltpu.VMEM((slab_count, span_x * 8, width), f32),
            pltpu.VMEM((3 * span_x * 8, width), bf16),
            pltpu.VMEM((3, 2 * pair_list.shape[1], TILE), f32),
            pltpu.VMEM((4, 8, TILE), f32),
            pltpu.VMEM((4, 8, TILE), f32),
            sems((4,)),
            sems((4,)),
            sems((column_count,)),
            sems((column_count,)),
            sems((slab_count,)),
            sems((slab_count,)),
            sems((4,)),
            sems((4,)),
        ],
        compiler_params=pltpu.CompilerParams(
            collective_id=0, has_side_effects=True, vmem_limit_bytes=40 * 1024 * 1024
        ),
        name="dislocation_forces",
    )(
        seg_ends,
        burgers,
        cell_index.reshape(1, seg_count),
        send_list,
        pair_list,
        pair_list,
        coupling,
        columns,
        slabs,
    )


def solution(mesh):
    placed = (
        P(None, ("gx", "yz")),
        P(None, ("gx", "yz")),
        P(("gx", "yz")),
        P(None, ("gx", "yz")),
        P(None, ("gx", "yz")),
        P(),
    )
    return jax.shard_map(
        on_device, mesh=mesh, in_specs=placed, out_specs=P(None, ("gx", "yz")), check_vma=False
    )
```

time: 218 us -> 39.6 us (0.18)
  other arithmetic: 108 us -> 0 us
  local copies, waits for them, and re-layouts: 42.7 us -> 7.08 us
  Pallas kernels: 0 us -> 32.2 us
  waiting for transfers between devices: 22.5 us -> 0 us
  matrix products: 15.2 us -> 0 us
  starting transfers between devices: 14.2 us -> 0 us
  between operations: 13.8 us -> 0.02 us
    reduce_sum x48 -> x0, other arithmetic: 65.7 us -> none  [the longest x16 32.4 us: pair_block(): on_source = -jnp.sum(pushed, axis=2) * distinct[:, None, None]]
    pallas_call x0 -> x1, Pallas kernels: none -> 32.2 us  [on_device(): pl.pallas_call(functools.partial(body, span_x, span_y, slab_count, column...]
    gather x36 -> x0, local copies, waits for them, and re-layouts: 30.6 us -> none  [the longest x2 11.4 us: on_device(): jnp.take(stress, cell_index, axis=1)]
    scatter-add x2 -> x0, other arithmetic: 26.8 us -> none  [the longest x1 22.5 us: on_device(): jax.ops.segment_sum(moment_terms.T, cell_index, num_segments=owned)]
    psum x1 -> x0, waiting for transfers between devices: 21.2 us -> none  [on_device(): full_grid = lax.psum(placed, ('gx', 'yz'))]
    dot_general x36 -> x0, matrix products: 15.2 us -> none  [the longest x16 4.8 us: pair_block(): jnp.einsum('pn,pct->nct', source_hot, on_source, precision=high)]
    ppermute x8 -> x0, starting transfers between devices: 14.1 us -> none  [passed_along(): return lax.ppermute(x, axis, [(i, (i + by) % count) for i in range(count)])]
    mul x18 -> x0, other arithmetic: 8.25 us -> none  [the longest x16 7.34 us: pair_block(): weight = weight * usable[:, None, None].astype(jnp.float32)]
  transfers between devices with their start and end apart: 9 -> 0, of which waited for: 3 -> 0; matrix products, arithmetic and copies ran while one was open for 50% -> 0% of each run, Pallas kernels for 0% -> 0%
where the time goes in v1:
time: 39.6 us; the launch traced here: 39.3 us
  Pallas kernels  32.2 us (81%)
  local copies, waits for them, and re-layouts  7.08 us (18%)
    pallas_call x1, Pallas kernels, on_device(): pl.pallas_call(functools.partial(body, span_x, span_y, slab_count, column...  32.2 us
    unnamed x17, local copies, waits for them, and re-layouts  7.08 us

profile of v1, /device:TPU:0, one launch (start us, length us, event | category | flops | bytes accessed | tf_op | source)
XLA Modules:
  0.0 39.3 jit_solution(485075280154986749)
XLA Ops:
  0.0 0.0 copy-start
  0.0 1.0 %copy-done = f32[8,128,128]{2,1,0:T(8,128)S(1)} copy-done((f32[8,128,128]{2,1,0:T(8,128)S(1)}, f32[8,128,128]{2,1,0:T(8,128)}, u32[]{:S(2)}) %copy-start) | copy-done | bytes 524312
  1.0 0.0 copy-start.1
  1.0 0.9 %copy-done.1 = f32[6,4096]{1,0:T(8,128)S(1)} copy-done((f32[6,4096]{1,0:T(8,128)S(1)}, f32[6,4096]{1,0:T(8,128)}, u32[]{:S(2)}) %copy-start.1) | copy-done | bytes 98328
  1.9 0.0 copy-start.2
  1.9 0.9 %copy-done.2 = f32[4,64,64]{2,1,0:T(8,128)S(1)} copy-done((f32[4,64,64]{2,1,0:T(8,128)S(1)}, f32[4,64,64]{2,1,0:T(8,128)}, u32[]{:S(2)}) %copy-start.2) | copy-done | bytes 65560
  2.9 0.0 copy-start.3
  2.9 0.8 %copy-done.3 = f32[3,4096]{1,0:T(4,128)S(1)} copy-done((f32[3,4096]{1,0:T(4,128)S(1)}, f32[3,4096]{1,0:T(4,128)}, u32[]{:S(2)}) %copy-start.3) | copy-done | bytes 49176
  3.7 0.0 copy-start.4
  3.7 0.7 %copy-done.4 = s32[4096]{0:T(1024)S(1)} copy-done((s32[4096]{0:T(1024)S(1)}, s32[4096]{0:T(1024)}, u32[]{:S(2)}) %copy-start.4) | copy-done | bytes 16408
  4.4 0.0 copy-start.5
  4.4 0.7 %copy-done.5 = s32[2,256]{1,0:T(2,128)S(1)} copy-done((s32[2,256]{1,0:T(2,128)S(1)}, s32[2,256]{1,0:T(2,128)}, u32[]{:S(2)}) %copy-start.5) | copy-done | bytes 2072
  5.1 0.0 copy-start.6
  5.1 0.7 %copy-done.6 = f32[6,9]{1,0:T(8,128)S(1)} copy-done((f32[6,9]{1,0:T(8,128)S(1)}, f32[6,9]{1,0:T(8,128)}, u32[]{:S(2)}) %copy-start.6) | copy-done | bytes 240
  5.8 0.0 copy-start.7
  5.8 0.7 %copy-done.7 = s32[4,128]{1,0:T(4,128)S(1)} copy-done((s32[4,128]{1,0:T(4,128)S(1)}, s32[4,128]{1,0:T(4,128)}, u32[]{:S(2)}) %copy-start.7) | copy-done | bytes 2072
  6.5 32.2 %dislocation_forces.1 = f32[3,4096]{1,0:T(4,128)S(1)} custom-call(f32[6,4096]{1,0:T(8,128)S(1)} %copy-done.1, f32[3,4096]{1,0:T(4,128)S(1)} %copy-done.3, s32[1,4096]{1,0:T(1,128)S(1)} %bitcast.1, s32[4,128]{1,0:T(4,128)S(1)} %copy-done.7, s32[2,256]{1,0:T(2,128)S(1)} %copy-done.5, s32[2,256]{1,0:T(2,128)S(1)} %copy-done.5, f32[6,9]{1,0:T(8,128)S(1)} %copy-done.6, ...), custom_call_target="tpu_custom_call" | custom-call | tf_op jit(solution)/shard_map/dislocation_forces/pallas_call | solution.py:376
  38.6 0.6 %copy.10 = f32[3,4096]{1,0:T(4,128)} copy(f32[3,4096]{1,0:T(4,128)S(1)} %dislocation_forces.1) | data formatting | bytes 98304
Async XLA Ops:
  0.0 1.0 %copy-start = (f32[8,128,128]{2,1,0:T(8,128)S(1)}, f32[8,128,128]{2,1,0:T(8,128)}, u32[]{:S(2)}) copy-start(f32[8,128,128]{2,1,0:T(8,128)} %constant.4.clone.column_ref) | copy-start | bytes 1572868
  1.0 0.9 %copy-start.1 = (f32[6,4096]{1,0:T(8,128)S(1)}, f32[6,4096]{1,0:T(8,128)}, u32[]{:S(2)}) copy-start(f32[6,4096]{1,0:T(8,128)} %seg_ref.1) | copy-start | bytes 294916
  1.9 0.9 %copy-start.2 = (f32[4,64,64]{2,1,0:T(8,128)S(1)}, f32[4,64,64]{2,1,0:T(8,128)}, u32[]{:S(2)}) copy-start(f32[4,64,64]{2,1,0:T(8,128)} %constant.5.clone.slab_ref) | copy-start | bytes 196612
  2.9 0.8 %copy-start.3 = (f32[3,4096]{1,0:T(4,128)S(1)}, f32[3,4096]{1,0:T(4,128)}, u32[]{:S(2)}) copy-start(f32[3,4096]{1,0:T(4,128)} %burgers_ref.1) | copy-start | bytes 147460
  3.7 0.7 %copy-start.4 = (s32[4096]{0:T(1024)S(1)}, s32[4096]{0:T(1024)}, u32[]{:S(2)}) copy-start(s32[4096]{0:T(1024)} %param.10) | copy-start | bytes 49156
  4.4 0.7 %copy-start.5 = (s32[2,256]{1,0:T(2,128)S(1)}, s32[2,256]{1,0:T(2,128)}, u32[]{:S(2)}) copy-start(s32[2,256]{1,0:T(2,128)} %pair_smem.1) | copy-start | bytes 6148
  5.1 0.7 %copy-start.6 = (f32[6,9]{1,0:T(8,128)S(1)}, f32[6,9]{1,0:T(8,128)}, u32[]{:S(2)}) copy-start(f32[6,9]{1,0:T(8,128)} %coupling_ref.1) | copy-start | bytes 652
  5.8 0.7 %copy-start.7 = (s32[4,128]{1,0:T(4,128)S(1)}, s32[4,128]{1,0:T(4,128)}, u32[]{:S(2)}) copy-start(s32[4,128]{1,0:T(4,128)} %send_ref.1) | copy-start | bytes 6148

commit v2 on v1

--- a/solution.py
+++ b/solution.py
@@ -74,6 +74,15 @@
     span_y,
     slab_count,
     column_count,
+    seg_hbm,
+    burgers_hbm,
+    cell_hbm,
+    send_hbm,
+    pair_hbm,
+    coupling_hbm,
+    column_hbm,
+    slab_hbm,
+    out_ref,
     seg_ref,
     burgers_ref,
     cell_ref,
@@ -83,7 +92,6 @@
     coupling_ref,
     column_ref,
     slab_ref,
-    out_ref,
     raw,
     ghost_out,
     ghost_in,
@@ -106,6 +114,7 @@
     slab_recv,
     return_send,
     return_recv,
+    load_sem,
 ):
     seg_count = seg_ref.shape[1]
     local_tiles = seg_count // TILE
@@ -121,6 +130,22 @@
     def column_peer(by):
         return (gx, lax.rem(yz + by, column_count))
 
+    loads = []
+    for source, destination in (
+        (seg_hbm, seg_ref),
+        (burgers_hbm, burgers_ref),
+        (send_hbm, send_ref),
+        (cell_hbm, cell_ref),
+        (coupling_hbm, coupling_ref),
+        (pair_hbm, pair_smem),
+        (pair_hbm, pair_ref),
+        (column_hbm, column_ref),
+        (slab_hbm, slab_ref),
+    ):
+        load = pltpu.make_async_copy(source, destination, load_sem.at[len(loads)])
+        load.start()
+        loads.append(load)
+
     barrier = pltpu.get_barrier_semaphore()
     for by in range(1, slab_count):
         pl.semaphore_signal(barrier, inc=1, device_id=slab_peer(by), device_id_type=MESH)
@@ -128,6 +153,8 @@
         pl.semaphore_signal(barrier, inc=1, device_id=column_peer(by), device_id_type=MESH)
 
     raw[...] = jnp.zeros_like(raw)
+    for load in loads[0:3]:
+        load.wait()
     for tile in range(local_tiles):
         at = slice(tile * TILE, (tile + 1) * TILE)
         raw[tile, 0:3] = 0.5 * (seg_ref[0:3, at] + seg_ref[3:6, at])
@@ -169,6 +196,8 @@
         ghost_copies.append(copy)
 
     moments[...] = jnp.zeros_like(moments)
+    for load in loads[3:5]:
+        load.wait()
 
     @pl.loop(0, seg_count // CHUNK)
     def _(step):
@@ -267,6 +296,8 @@
                 for c in range(3):
                     pushed[c, pl.ds(side * pair_count + base + k, 1)] = force[c : c + 1]
 
+    for load in loads[5:9]:
+        load.wait()
     steps = pair_count // TOGETHER
     pl.loop(0, steps // 2)(pairs)
 
@@ -371,14 +402,22 @@
     slabs = jnp.asarray(slab_matrices(slab_count, span_x))
     width = columns.shape[1]
     vmem = pl.BlockSpec(memory_space=pltpu.VMEM)
-    smem = pl.BlockSpec(memory_space=pltpu.SMEM)
     sems = pltpu.SemaphoreType.DMA
     return pl.pallas_call(
         functools.partial(body, span_x, span_y, slab_count, column_count),
         out_shape=jax.ShapeDtypeStruct((3, seg_count), f32),
-        in_specs=[vmem] * 5 + [smem] + [vmem] * 3,
+        in_specs=[pl.BlockSpec(memory_space=pltpu.HBM)] * 8,
         out_specs=vmem,
         scratch_shapes=[
+            pltpu.VMEM(seg_ends.shape, f32),
+            pltpu.VMEM(burgers.shape, f32),
+            pltpu.VMEM((1, seg_count), jnp.int32),
+            pltpu.VMEM(send_list.shape, jnp.int32),
+            pltpu.VMEM(pair_list.shape, jnp.int32),
+            pltpu.SMEM(pair_list.shape, jnp.int32),
+            pltpu.VMEM(coupling.shape, f32),
+            pltpu.VMEM(columns.shape, f32),
+            pltpu.VMEM(slabs.shape, f32),
             pltpu.VMEM((tiles - 4 + 4, 16, TILE), f32),
             pltpu.VMEM((4, 16, TILE), f32),
             pltpu.VMEM((4, 16, TILE), f32),
@@ -401,9 +440,10 @@
             sems((slab_count,)),
             sems((4,)),
             sems((4,)),
+            sems((9,)),
         ],
         compiler_params=pltpu.CompilerParams(
-            collective_id=0, has_side_effects=True, vmem_limit_bytes=40 * 1024 * 1024
+            collective_id=0, has_side_effects=True, vmem_limit_bytes=64 * 1024 * 1024
         ),
         name="dislocation_forces",
     )(
@@ -411,7 +451,6 @@
         burgers,
         cell_index.reshape(1, seg_count),
         send_list,
-        pair_list,
         pair_list,
         coupling,
         columns,

time: 39.6 us -> 34 us (0.86)
  local copies, waits for them, and re-layouts: 7.08 us -> 1.48 us
    unnamed x17 -> x1, local copies, waits for them, and re-layouts: 7.08 us -> 1.48 us
where the time goes in v2:
time: 34 us; the launch traced here: 33.8 us
  Pallas kernels  32.3 us (95%)
  local copies, waits for them, and re-layouts  1.48 us (4%)
    pallas_call x1, Pallas kernels, on_device(): pl.pallas_call(functools.partial(body, span_x, span_y, slab_count, column...  32.3 us
    unnamed x1, local copies, waits for them, and re-layouts  1.48 us

profile of v2, /device:TPU:0, one launch (start us, length us, event | category | flops | bytes accessed | tf_op | source)
XLA Modules:
  0.0 33.8 jit_solution(17954953470776699523)
XLA Ops:
  0.0 32.3 %dislocation_forces.1 = f32[3,4096]{1,0:T(4,128)} custom-call(f32[6,4096]{1,0:T(8,128)} %seg_hbm.1, f32[3,4096]{1,0:T(4,128)} %burgers_hbm.1, s32[1,4096]{1,0:T(1,128)} %bitcast.1, s32[4,128]{1,0:T(4,128)} %send_hbm.1, s32[2,256]{1,0:T(2,128)} %pair_hbm.1, f32[6,9]{1,0:T(8,128)} %coupling_hbm.1, f32[8,128,128]{2,1,0:T(8,128)} %constant.4.clone.column_hbm, ...), custom_call_target="tpu_custom_call" | custom-call | tf_op jit(solution)/shard_map/dislocation_forces/pallas_call | solution.py:406
  32.3 1.5 %copy.10 = f32[3,4096]{1,0:T(4,128)} copy(f32[3,4096]{1,0:T(4,128)} %dislocation_forces.1) | data formatting | bytes 98304
